TPU v7x, 32 devices: a whole 2x2x4 slice. The times are simulated.
32 devices in a mesh: fsdp: 16 (over z, y, x), replica: 2 (over core).
Axes of the slice: x: 2, y: 2, z: 4, core: 2. Of those that a mesh axis runs over, the one named last changes fastest.
Arguments:
- partials: float32 [2, 16384, 128], P('replica', 'fsdp'), may hold values from -6 to 6
- diag_stat: float32 [16384, 128], P('fsdp'), may hold values from 0.8 to 3
- first_stat: float32 [16384, 128], P('fsdp'), may hold values from -0.35 to 0.35
- second_stat: float32 [16384, 128], P('fsdp'), may hold values from -0.35 to 0.35
Outputs:
- update: float32 [16384, 128], P('fsdp')
- diag_next: float32 [16384, 128], P('fsdp')
- first_next: float32 [16384, 128], P('fsdp')
- second_next: float32 [16384, 128], P('fsdp')
All inputs are finite; a program needn't handle non-finite values.
Results may differ from a plain program's by a relative error of at most 0.00002.
Values sent between devices are 32-bit elements; how exact they have to be, the bound alone decides.
No kernel may reach another device: no remote copies, remote signals or barrier semaphores. Data moves between devices by JAX's collectives and lax.ppermute only.
A program may use at most 64 MiB of HBM per device.

v0:
```python
import functools

import jax
import jax.numpy as jnp
from jax import lax
from jax.experimental import pallas as pl
from jax.experimental.pallas import tpu as pltpu
from jax.sharding import PartitionSpec as P

decay_rate = 0.95
damping = 0.01
PAD = 8
TILE = 8


def solved(g, g1, g2, d, upper, lower, f, c, s):
    det = upper * lower - c * c
    n1 = lower * f - c * s
    n2 = upper * s - c * f
    schur = d * det - f * n1 - s * n2
    top = g * det - n1 * g1 - n2 * g2
    w = top / (schur * det)
    return w * det, w * n1, w * n2


def collect(rows, own, diag, first, second, out, tiles, sems):
    even = lax.rem(lax.axis_index("fsdp"), 2) == 0
    at = pl.multiple_of(jnp.where(even, 0, rows - TILE), TILE)
    copies = [
        pltpu.make_async_copy(
            source.at[pl.ds(at, TILE), :], tiles.at[k * TILE : (k + 1) * TILE, :], sems.at[k]
        )
        for k, source in enumerate((own, diag, first, second))
    ]
    for copy in copies:
        copy.start()
    for copy in copies:
        copy.wait()

    @pl.when(even)
    def _():
        for k in range(3):
            out[2 * k : 2 * k + 2, :] = tiles[k * TILE : k * TILE + 2, :]
        out[6:8, :] = jnp.ones((2, out.shape[1]), jnp.float32)

    @pl.when(jnp.logical_not(even))
    def _():
        for k in range(4):
            out[2 * k : 2 * k + 2, :] = tiles[(k + 1) * TILE - 2 : (k + 1) * TILE, :]


def ready(scale, rows, own, other, diag, first, second, out):
    even = lax.rem(lax.axis_index("fsdp"), 2) == 0

    def fill(at, sources):
        out[0:2, :] = (own[at : at + 2, :] + other[at : at + 2, :]) * scale
        for k, source in enumerate(sources):
            out[2 * k + 2 : 2 * k + 4, :] = source[at : at + 2, :]

    @pl.when(even)
    def _():
        fill(rows - 2, (diag, first, second))

    @pl.when(jnp.logical_not(even))
    def _():
        fill(0, (diag, first))
        out[6:8, :] = jnp.ones((2, out.shape[1]), jnp.float32)


def interior(parts, early, scale, rows, chunk, step, *refs):
    chosen = lax.axis_index("fsdp") == 0
    pl.when(chosen if early else jnp.logical_not(chosen))(
        functools.partial(
            everything, parts, scale, rows, chunk, step, *refs[: parts + 3], *refs[-12:]
        )
    )


def everything(parts, scale, rows, chunk, step, *refs):
    pieces = refs[:parts]
    diag_in, first_in, second_in = refs[parts : parts + 3]
    outs = refs[parts + 3 : parts + 6]
    update, edges = refs[parts + 6 : parts + 8]
    grad, diag, first, second, part1, part2, sems = refs[parts + 8 :]
    width = edges.shape[1]
    end = PAD + rows
    chunks = rows // chunk

    zeros = jnp.zeros((PAD, width), jnp.float32)
    grad[end:, :] = zeros
    diag[end:, :] = zeros + 1.0
    first[end:, :] = zeros
    part1[:PAD, :] = zeros
    part2[:PAD, :] = zeros

    def gradients(at, size):
        here, there = pl.ds(at, size), pl.ds(at + PAD, size)
        g = pieces[0][here, :]
        for piece in pieces[1:]:
            g = g + piece[here, :]
        g = g * scale
        grad[there, :] = g
        diag[there, :] = decay_rate * diag_in[here, :] + g * g

    def bands(at, size):
        here, there = pl.ds(at, size), pl.ds(at + PAD, size)
        g = grad[there, :]
        g1 = grad[pl.ds(at + PAD + 1, size), :]
        g2 = grad[pl.ds(at + PAD + 2, size), :]
        first[there, :] = decay_rate * first_in[here, :] + g * g1
        second[there, :] = decay_rate * second_in[here, :] + g * g2

    def values(at, size):
        there = pl.ds(at + PAD, size)
        after = pl.ds(at + PAD + 1, size)
        later = pl.ds(at + PAD + 2, size)
        v, p1, p2 = solved(
            grad[there, :],
            grad[after, :],
            grad[later, :],
            diag[there, :] + damping,
            diag[after, :] + damping,
            diag[later, :] + damping,
            first[there, :],
            first[after, :],
            second[there, :],
        )
        part1[there, :] = p1
        part2[there, :] = p2
        update[pl.ds(at, size), :] = (
            v - part1[pl.ds(at + PAD - 1, size), :] - part2[pl.ds(at + PAD - 2, size), :]
        )

    def over(work, low, high):
        for at in range(low, high, step):
            work(at, min(step, high - at))

    stores = []

    def send(source, k, c, low, high):
        copy = pltpu.make_async_copy(
            source.at[low + PAD : high + PAD, :], outs[k].at[low:high, :], sems.at[k, c]
        )
        copy.start()
        stores.append(copy)

    for c in range(chunks):
        low, high = c * chunk, (c + 1) * chunk
        over(gradients, low, high)
        send(diag, 0, c, low, high)
        low, high = max(low - TILE, 0), high if c == chunks - 1 else high - TILE
        over(bands, low, high)
        send(first, 1, c, low, high)
        send(second, 2, c, low, high)
    over(values, 0, rows)

    tops = [grad[PAD : PAD + TILE, :], diag[PAD : PAD + TILE, :], first[PAD : PAD + TILE, :]]
    tops.append(update[:TILE, :])
    tails = [r[end - TILE : end, :] for r in (grad, diag, first, second)]
    tails.append(update[rows - TILE :, :])
    tails += [r[end - TILE : end, :] for r in (part1, part2)]
    for k, tile in enumerate(tops + tails):
        edges[k * TILE : (k + 1) * TILE, :] = tile
    for copy in stores:
        copy.wait()


def store(rows, chunk, update, out, sems):
    copies = []
    for c in range(rows // chunk):
        low, high = max(c * chunk, TILE), min((c + 1) * chunk, rows - TILE)
        copies.append(
            pltpu.make_async_copy(update.at[low:high, :], out.at[low:high, :], sems.at[c])
        )
    for copy in copies:
        copy.start()
    for copy in copies:
        copy.wait()


def border(rows, shards, scale, turn, *refs):
    chosen = lax.axis_index("fsdp") == 0
    if turn == 0:
        patch(rows, shards, scale, *refs)
    else:
        pl.when(chosen if turn == 1 else jnp.logical_not(chosen))(
            functools.partial(patch, rows, shards, scale, *refs)
        )


def patch(rows, shards, scale, *refs):
    edges, near, far, other = refs[:4]
    outs = refs[7:10]
    work, tiles, sems = refs[10:]

    def edge(k, at, size):
        return edges[k * TILE + at : k * TILE + at + size, :]

    shard = lax.axis_index("fsdp")
    even = lax.rem(shard, 2) == 0
    near_rows, far_rows = near[...], far[...]
    if scale != 1.0:
        far_sum = (far_rows[0:2] + other[0:2, :]) * scale
        far_rows = jnp.concatenate([far_sum, far_rows[2:8]])
    before = jnp.where(even, far_rows, near_rows)
    after = jnp.where(even, near_rows, far_rows)
    work[0:8, :] = jnp.where(shard == 0, 0.0, before)
    work[8:16, :] = jnp.where(shard == shards - 1, 0.0, after)

    g = work[0:2, :]
    g_next = edge(0, 0, 2)
    d = decay_rate * work[2:4, :] + g * g + damping
    d_next = edge(1, 0, 2) + damping
    g1 = jnp.concatenate([g[1:2], g_next[0:1]])
    d1 = jnp.concatenate([d[1:2], d_next[0:1]])
    f = decay_rate * work[4:6, :] + g * g1
    s = decay_rate * work[6:8, :] + g * g_next
    c = jnp.concatenate([f[1:2], edge(2, 0, 1)])
    _, p1, p2 = solved(g, g1, g_next, d, d1, d_next, f, c, s)
    tiles[0:8, :] = edges[3 * TILE : 4 * TILE, :]
    tiles[0:1, :] = tiles[0:1, :] - p1[1:2] - p2[0:1]
    tiles[1:2, :] = tiles[1:2, :] - p2[1:2]

    g = edge(4, 6, 2)
    g_next = work[8:10, :]
    present = work[14:16, :]
    d = edge(5, 6, 2) + damping
    d_next = (
        decay_rate * work[10:12, :] + g_next * g_next + present * damping + (1.0 - present)
    )
    g1 = jnp.concatenate([g[1:2], g_next[0:1]])
    d1 = jnp.concatenate([d[1:2], d_next[0:1]])
    f_last = (edge(6, 7, 1) + g[1:2] * g_next[0:1]) * present[0:1]
    f = jnp.concatenate([edge(6, 6, 1), f_last])
    s = (edge(7, 6, 2) + g * g_next) * present
    f_next = decay_rate * work[12:13, :] + g_next[0:1] * g_next[1:2]
    c = jnp.concatenate([f_last, f_next])
    v, p1, _ = solved(g, g1, g_next, d, d1, d_next, f, c, s)
    tiles[8:16, :] = edges[8 * TILE : 9 * TILE, :]
    tiles[14:15, :] = v[0:1] - edge(9, 5, 1) - edge(10, 4, 1)
    tiles[15:16, :] = v[1:2] - p1[0:1] - edge(10, 5, 1)
    tiles[16:24, :] = edges[6 * TILE : 7 * TILE, :]
    tiles[23:24, :] = f_last
    tiles[24:32, :] = edges[7 * TILE : 8 * TILE, :]
    tiles[30:32, :] = s

    copies = [
        pltpu.make_async_copy(tiles.at[0:8, :], outs[0].at[0:TILE, :], sems.at[0]),
        pltpu.make_async_copy(tiles.at[8:16, :], outs[0].at[rows - TILE : rows, :], sems.at[1]),
        pltpu.make_async_copy(tiles.at[16:24, :], outs[1].at[rows - TILE : rows, :], sems.at[2]),
        pltpu.make_async_copy(tiles.at[24:32, :], outs[2].at[rows - TILE : rows, :], sems.at[3]),
    ]
    for copy in copies:
        copy.start()
    for copy in copies:
        copy.wait()


def trades(shards, low):
    partner = {}
    for i in range(low, shards - 1, 2):
        partner[i], partner[i + 1] = i + 1, i
    return [
        (2 * i + core, 2 * partner.get(i, i) + 1 - core) for i in range(shards) for core in range(2)
    ]


def body(partials, diag_stat, first_stat, second_stat):
    own = partials[0]
    rows, width = own.shape
    replicas = lax.axis_size("replica")
    shards = lax.axis_size("fsdp")
    scale = 1.0 / replicas
    axes = ("fsdp", "replica")
    paired = replicas == 2 and shards > 1

    shape = jax.ShapeDtypeStruct((rows, width), jnp.float32)
    vmem = pl.BlockSpec(memory_space=pltpu.VMEM)
    hbm = pl.BlockSpec(memory_space=pl.ANY)
    params = pltpu.CompilerParams(vmem_limit_bytes=24 * 2**20)

    def swap(block):
        return lax.ppermute(block, "replica", [(0, 1), (1, 0)])

    def stay(block):
        return pltpu.with_memory_space_constraint(block, pltpu.HBM)

    stats = (diag_stat, first_stat, second_stat)
    tile = pltpu.VMEM((TILE, width), jnp.float32)
    if paired:
        pieces = [own, swap(own)]
        far = pl.pallas_call(
            functools.partial(collect, rows),
            out_shape=tile,
            in_specs=[hbm] * 4,
            out_specs=vmem,
            scratch_shapes=[
                pltpu.VMEM((4 * TILE, width), jnp.float32),
                pltpu.SemaphoreType.DMA((4,)),
            ],
            compiler_params=params,
            name="collect",
        )(*[stay(x) for x in (own, *stats)])
        far = lax.ppermute(far, axes, trades(shards, 1))
    else:
        pieces = [lax.psum(own, "replica") * scale]
        scale = 1.0
        tail = rows - 2
        ones = jnp.ones((2, width), jnp.float32)
        last = jnp.concatenate([x[tail:] for x in (*pieces, *stats)])
        head = jnp.concatenate([x[:2] for x in (*pieces, *stats[:2])] + [ones])
        before = lax.ppermute(last, "fsdp", [(i, i + 1) for i in range(shards - 1)])
        after = lax.ppermute(head, "fsdp", [(i + 1, i) for i in range(shards - 1)])
        even = lax.axis_index("fsdp") % 2 == 0
        near, far = jnp.where(even, after, before), jnp.where(even, before, after)

    parts = len(pieces)
    whole = pltpu.VMEM((rows, width), jnp.float32)
    padded = pltpu.VMEM((rows + 2 * PAD, width), jnp.float32)
    chunk = 256 if rows % 256 == 0 else rows
    inner = [pltpu.with_memory_space_constraint(x, pltpu.VMEM) for x in (*pieces, *stats)]

    def inside(early, *done):
        return pl.pallas_call(
            functools.partial(interior, parts, early, scale, rows, chunk, 64),
            out_shape=(shape,) * 3 + (whole, pltpu.VMEM((11 * TILE, width), jnp.float32)),
            in_specs=[vmem] * (parts + 3) + ([hbm] * 3 + [vmem] * 2 if done else []),
            out_specs=(hbm,) * 3 + (vmem,) * 2,
            input_output_aliases={parts + 3 + k: k for k in range(len(done))},
            scratch_shapes=[padded] * 6 + [pltpu.SemaphoreType.DMA((3, rows // chunk))],
            compiler_params=params,
            cost_estimate=pl.CostEstimate(
                flops=45 * rows * width, bytes_accessed=36 * rows * width, transcendentals=0
            ),
            name="early" if early else "late",
        )(*inner, *done)

    done = inside(True)
    if paired:
        near = pl.pallas_call(
            functools.partial(ready, scale, rows),
            out_shape=tile,
            in_specs=[vmem] * 5,
            out_specs=vmem,
            compiler_params=params,
            name="ready",
        )(*inner)
        near, *done = lax.optimization_barrier((near, *done))
        near = lax.ppermute(near, axes, trades(shards, 0))
    diag_next, first_next, second_next, update, edges = inside(False, *done)
    other = far
    if paired:
        far, edges = lax.optimization_barrier((far, edges))
        other = swap(far)
    update = pl.pallas_call(
        functools.partial(store, rows, chunk),
        out_shape=shape,
        in_specs=[vmem],
        out_specs=hbm,
        scratch_shapes=[pltpu.SemaphoreType.DMA((rows // chunk,))],
        compiler_params=params,
        cost_estimate=pl.CostEstimate(
            flops=0, bytes_accessed=8 * rows * width, transcendentals=0
        ),
        name="store",
    )(pltpu.with_memory_space_constraint(update, pltpu.VMEM))

    def patched(turn, other, *done):
        return pl.pallas_call(
            functools.partial(border, rows, shards, scale, turn),
            out_shape=(shape,) * 3,
            in_specs=[vmem] * 4 + [hbm] * 3,
            out_specs=(hbm,) * 3,
            input_output_aliases={4: 0, 5: 1, 6: 2},
            scratch_shapes=[
                pltpu.VMEM((16, width), jnp.float32),
                pltpu.VMEM((32, width), jnp.float32),
                pltpu.SemaphoreType.DMA((4,)),
            ],
            compiler_params=params,
            name="border",
        )(edges, near, far, other, *done)

    if paired:
        done = patched(1, far, update, first_next, second_next)
        update, first_next, second_next = patched(2, other, *done)
    else:
        update, first_next, second_next = patched(0, far, update, first_next, second_next)
    return update, diag_next, first_next, second_next


def solution(mesh):
    return jax.shard_map(
        body,
        mesh=mesh,
        in_specs=(P("replica", "fsdp", None), P("fsdp", None), P("fsdp", None), P("fsdp", None)),
        out_specs=(P("fsdp", None), P("fsdp", None), P("fsdp", None), P("fsdp", None)),
        check_vma=False,
    )
```

profile of v0, /device:TPU:9, one launch (start us, length us, event | category | flops | bytes accessed | tf_op | source)
XLA Modules:
  0.0 8.9 jit_solution(18102745475653105620)
XLA Ops:
  0.6 0.0 copy-start
  0.6 0.0 copy-start.1
  0.7 0.0 copy-start.2
  0.7 0.0 copy-start.3
  0.7 0.7 %collective-permute-start.1 = (f32[1024,128]{1,0:T(8,128)}, f32[1024,128]{1,0:T(8,128)S(1)}, u32[]{:S(2)}, u32[]{:S(2)}) collective-permute-start(f32[1024,128]{1,0:T(8,128)} %bitcast.1), channel_id=1, source_target_pairs={{0,1},{1,0},{2,3},{3,2},{4,5},{5,4},{6,7},{7,6},{8,9},{9,8},{10,11... | collective-permute-start | bytes 1572872 | tf_op jit(solution)/shard_map/ppermute | solution.py:283
  1.4 0.8 %collect.1 = f32[8,128]{1,0:T(8,128)S(1)} custom-call(f32[1024,128]{1,0:T(8,128)} %bitcast.2, f32[1024,128]{1,0:T(8,128)} %refs_2_.3, f32[1024,128]{1,0:T(8,128)} %refs_3_.3, f32[1024,128]{1,0:T(8,128)} %refs_4_.3), custom_call_target="tpu_custom_call" | custom-call | tf_op jit(solution)/shard_map/collect/pallas_call | solution.py:292
  2.2 2.2 %collective-permute-start = (f32[8,128]{1,0:T(8,128)S(1)}, f32[8,128]{1,0:T(8,128)S(1)}, u32[]{:S(2)}, u32[]{:S(2)}) collective-permute-start(f32[8,128]{1,0:T(8,128)S(1)} %collect.1), channel_id=1, source_target_pairs={{0,1},{1,0},{2,5},{3,4},{4,3},{5,2},{6,9},{7,8},{8,7},{9,6},{10,13... | collective-permute-start | bytes 12296 | tf_op jit(solution)/shard_map/ppermute | solution.py:304
  4.4 0.0 collective-permute-done.1.other.refs_1_
  4.4 0.0 copy-done
  4.4 0.0 copy-done.1
  4.4 0.0 copy-done.2
  4.4 0.0 copy-done.3
  4.4 0.1 %early.1 = (f32[1024,128]{1,0:T(8,128)}, f32[1024,128]{1,0:T(8,128)}, f32[1024,128]{1,0:T(8,128)}, f32[1024,128]{1,0:T(8,128)S(1)}, f32[88,128]{1,0:T(8,128)S(1)}) custom-call(f32[1024,128]{1,0:T(8,128)S(1)} %bitcast.4, f32[1024,128]{1,0:T(8,128)S(1)} %collective-permute-done.1.other.refs_1_, f32[1024,128]{1,0:T(8,128)S(1)} %copy-done.1, ...), custom_call_target="tpu_custom_call" | custom-call | flops 5898240 | bytes 4718592 | tf_op jit(solution)/shard_map/early/pallas_call | solution.py:324
  4.6 0.7 %collective-permute-start.2 = (f32[8,128]{1,0:T(8,128)S(1)}, f32[8,128]{1,0:T(8,128)S(1)}, u32[]{:S(2)}, u32[]{:S(2)}) collective-permute-start(f32[8,128]{1,0:T(8,128)S(1)} %ready.1), channel_id=1, source_target_pairs={{0,3},{1,2},{2,1},{3,0},{4,7},{5,6},{6,5},{7,4},{8,11},{9,10},{10,... | collective-permute-start | bytes 12296 | tf_op jit(solution)/shard_map/ppermute | solution.py:349
  5.2 1.3 %late.1 = (f32[1024,128]{1,0:T(8,128)}, f32[1024,128]{1,0:T(8,128)}, f32[1024,128]{1,0:T(8,128)}, f32[1024,128]{1,0:T(8,128)S(1)}, f32[88,128]{1,0:T(8,128)S(1)}) custom-call(f32[1024,128]{1,0:T(8,128)S(1)} %bitcast.5, ...), custom_call_target="tpu_custom_call", output_to_operand_aliasing={{0}: (5, {}), {1}: (6, {}), {2}: (7, {}), {3}: (8, {}), {4}... | custom-call | flops 5898240 | bytes 4718592 | tf_op jit(solution)/shard_map/late/pallas_call | solution.py:324
  6.5 0.6 %collective-permute-done.refs_2_.refs_3_ = f32[8,128]{1,0:T(8,128)S(1)} collective-permute-done((f32[8,128]{1,0:T(8,128)S(1)}, f32[8,128]{1,0:T(8,128)S(1)}, u32[]{:S(2)}, u32[]{:S(2)}) %collective-permute-start) | collective-permute-done | bytes 4128 | tf_op jit(solution)/shard_map/ppermute | solution.py:304
  7.1 0.2 %collective-permute-start.3 = (f32[8,128]{1,0:T(8,128)S(1)}, f32[8,128]{1,0:T(8,128)S(1)}, u32[]{:S(2)}, u32[]{:S(2)}) collective-permute-start(f32[8,128]{1,0:T(8,128)S(1)} %collective-permute-done.refs_2_.refs_3_), channel_id=1, source_target_pairs={{0,1},{1,0},{2,3},{3,2},{4,5},{5,4},{6,7},{7,6},{8,9},{9,8},{10,11... | collective-permute-start | bytes 12296 | tf_op jit(solution)/shard_map/ppermute | solution.py:283
  7.3 0.8 %store.1.refs_4_ = f32[1024,128]{1,0:T(8,128)} custom-call(f32[1024,128]{1,0:T(8,128)S(1)} %get-tuple-element.42.update), custom_call_target="tpu_custom_call" | custom-call | bytes 1048576 | tf_op jit(solution)/shard_map/store/pallas_call | solution.py:355
  8.1 0.0 collective-permute-done.2.refs_1_
  8.1 0.1 border.2
  8.1 0.1 %collective-permute-done.3.refs_3_ = f32[8,128]{1,0:T(8,128)S(1)} collective-permute-done((f32[8,128]{1,0:T(8,128)S(1)}, f32[8,128]{1,0:T(8,128)S(1)}, u32[]{:S(2)}, u32[]{:S(2)}) %collective-permute-start.3) | collective-permute-done | bytes 4128 | tf_op jit(solution)/shard_map/ppermute | solution.py:283
  8.3 0.7 %border.3 = (f32[1024,128]{1,0:T(8,128)}, f32[1024,128]{1,0:T(8,128)}, f32[1024,128]{1,0:T(8,128)}) custom-call(f32[88,128]{1,0:T(8,128)S(1)} %get-tuple-element.39.refs_0_, f32[8,128]{1,0:T(8,128)S(1)} %collective-permute-done.2.refs_1_, ...), custom_call_target="tpu_custom_call", output_to_operand_aliasing={{0}: (4, {}), {1}: (5, {}), {2}: (6, {})} | custom-call | tf_op jit(solution)/shard_map/border/pallas_call | solution.py:369
  (1 shorter events, 0.0 us)
Async XLA Ops:
  0.6 3.7 %copy-start = (f32[1,1024,128]{2,1,0:T(8,128)S(1)}, f32[1,1024,128]{2,1,0:T(8,128)}, u32[]{:S(2)}) copy-start(f32[1,1024,128]{2,1,0:T(8,128)} %param.4) | copy-start | bytes 1572868
  0.6 3.7 %copy-start.1 = (f32[1024,128]{1,0:T(8,128)S(1)}, f32[1024,128]{1,0:T(8,128)}, u32[]{:S(2)}) copy-start(f32[1024,128]{1,0:T(8,128)} %refs_2_.3) | copy-start | bytes 1572868
  0.7 3.7 %copy-start.2 = (f32[1024,128]{1,0:T(8,128)S(1)}, f32[1024,128]{1,0:T(8,128)}, u32[]{:S(2)}) copy-start(f32[1024,128]{1,0:T(8,128)} %refs_3_.3) | copy-start | bytes 1572868
  0.7 3.7 %copy-start.3 = (f32[1024,128]{1,0:T(8,128)S(1)}, f32[1024,128]{1,0:T(8,128)}, u32[]{:S(2)}) copy-start(f32[1024,128]{1,0:T(8,128)} %refs_4_.3) | copy-start | bytes 1572868
  0.7 3.7 %collective-permute-start.1 = (f32[1024,128]{1,0:T(8,128)}, f32[1024,128]{1,0:T(8,128)S(1)}, u32[]{:S(2)}, u32[]{:S(2)}) collective-permute-start(f32[1024,128]{1,0:T(8,128)} %bitcast.1), channel_id=1, source_target_pairs={{0,1},{1,0},{2,3},{3,2},{4,5},{5,4},{6,7},{7,6},{8,9},{9,8},{10,11... | collective-permute-start | bytes 1572872 | tf_op jit(solution)/shard_map/ppermute | solution.py:283
  2.2 4.9 %collective-permute-start = (f32[8,128]{1,0:T(8,128)S(1)}, f32[8,128]{1,0:T(8,128)S(1)}, u32[]{:S(2)}, u32[]{:S(2)}) collective-permute-start(f32[8,128]{1,0:T(8,128)S(1)} %collect.1), channel_id=1, source_target_pairs={{0,1},{1,0},{2,5},{3,4},{4,3},{5,2},{6,9},{7,8},{8,7},{9,6},{10,13... | collective-permute-start | bytes 12296 | tf_op jit(solution)/shard_map/ppermute | solution.py:304
  4.6 3.5 %collective-permute-start.2 = (f32[8,128]{1,0:T(8,128)S(1)}, f32[8,128]{1,0:T(8,128)S(1)}, u32[]{:S(2)}, u32[]{:S(2)}) collective-permute-start(f32[8,128]{1,0:T(8,128)S(1)} %ready.1), channel_id=1, source_target_pairs={{0,3},{1,2},{2,1},{3,0},{4,7},{5,6},{6,5},{7,4},{8,11},{9,10},{10,... | collective-permute-start | bytes 12296 | tf_op jit(solution)/shard_map/ppermute | solution.py:349
  7.1 1.2 %collective-permute-start.3 = (f32[8,128]{1,0:T(8,128)S(1)}, f32[8,128]{1,0:T(8,128)S(1)}, u32[]{:S(2)}, u32[]{:S(2)}) collective-permute-start(f32[8,128]{1,0:T(8,128)S(1)} %collective-permute-done.refs_2_.refs_3_), channel_id=1, source_target_pairs={{0,1},{1,0},{2,3},{3,2},{4,5},{5,4},{6,7},{7,6},{8,9},{9,8},{10,11... | collective-permute-start | bytes 12296 | tf_op jit(solution)/shard_map/ppermute | solution.py:283
where the time goes:
time: 9.08 us; the launch traced here: 8.93 us
  starting transfers between devices  3.74 us (41%)
  Pallas kernels  3.73 us (41%)
  between operations  0.74 us (8%)
  waiting for transfers between devices  0.71 us (8%)
    ppermute x1, starting transfers between devices, body(): far = lax.ppermute(far, axes, trades(shards, 1))  2.17 us
    pallas_call x2, Pallas kernels, inside(): pl.pallas_call(functools.partial(interior, parts, early, scale, rows, chu...  1.39 us
    ppermute x2, starting transfers between devices, swap(): return lax.ppermute(block, 'replica', [(0, 1), (1, 0)])  0.91 us
    pallas_call x1, Pallas kernels, body(): pl.pallas_call(functools.partial(store, rows, chunk), out_shape=shape, in...  0.81 us
    pallas_call x1, Pallas kernels, body(): pl.pallas_call(functools.partial(collect, rows), out_shape=tile, in_specs...  0.77 us
    pallas_call x2, Pallas kernels, patched(): pl.pallas_call(functools.partial(border, rows, shards, scale, turn), out_...  0.74 us
    ppermute x1, starting transfers between devices, body(): near = lax.ppermute(near, axes, trades(shards, 0))  0.66 us
    ppermute x1, waiting for transfers between devices, body(): far = lax.ppermute(far, axes, trades(shards, 1))  0.6 us
  transfers between devices with their start and end apart: 4, of which 2 were waited for; matrix products, arithmetic and copies ran while one was open for 0% of the time, Pallas kernels for 34%

commit v1 on v0

--- a/solution.py
+++ b/solution.py
@@ -41,7 +41,7 @@
     def _():
         for k in range(3):
             out[2 * k : 2 * k + 2, :] = tiles[k * TILE : k * TILE + 2, :]
-        out[6:8, :] = jnp.ones((2, out.shape[1]), jnp.float32)
+        out[6:8, :] = jnp.zeros((2, out.shape[1]), jnp.float32)
 
     @pl.when(jnp.logical_not(even))
     def _():
@@ -64,7 +64,7 @@
     @pl.when(jnp.logical_not(even))
     def _():
         fill(0, (diag, first))
-        out[6:8, :] = jnp.ones((2, out.shape[1]), jnp.float32)
+        out[6:8, :] = jnp.zeros((2, out.shape[1]), jnp.float32)
 
 
 def interior(parts, early, scale, rows, chunk, step, *refs):
@@ -191,58 +191,23 @@
 def patch(rows, shards, scale, *refs):
     edges, near, far, other = refs[:4]
     outs = refs[7:10]
-    work, tiles, sems = refs[10:]
-
-    def edge(k, at, size):
-        return edges[k * TILE + at : k * TILE + at + size, :]
-
-    shard = lax.axis_index("fsdp")
-    even = lax.rem(shard, 2) == 0
-    near_rows, far_rows = near[...], far[...]
-    if scale != 1.0:
-        far_sum = (far_rows[0:2] + other[0:2, :]) * scale
-        far_rows = jnp.concatenate([far_sum, far_rows[2:8]])
-    before = jnp.where(even, far_rows, near_rows)
-    after = jnp.where(even, near_rows, far_rows)
-    work[0:8, :] = jnp.where(shard == 0, 0.0, before)
-    work[8:16, :] = jnp.where(shard == shards - 1, 0.0, after)
-
-    g = work[0:2, :]
-    g_next = edge(0, 0, 2)
-    d = decay_rate * work[2:4, :] + g * g + damping
-    d_next = edge(1, 0, 2) + damping
-    g1 = jnp.concatenate([g[1:2], g_next[0:1]])
-    d1 = jnp.concatenate([d[1:2], d_next[0:1]])
-    f = decay_rate * work[4:6, :] + g * g1
-    s = decay_rate * work[6:8, :] + g * g_next
-    c = jnp.concatenate([f[1:2], edge(2, 0, 1)])
-    _, p1, p2 = solved(g, g1, g_next, d, d1, d_next, f, c, s)
+    tiles, sems = refs[10:]
     tiles[0:8, :] = edges[3 * TILE : 4 * TILE, :]
-    tiles[0:1, :] = tiles[0:1, :] - p1[1:2] - p2[0:1]
-    tiles[1:2, :] = tiles[1:2, :] - p2[1:2]
-
-    g = edge(4, 6, 2)
-    g_next = work[8:10, :]
-    present = work[14:16, :]
-    d = edge(5, 6, 2) + damping
-    d_next = (
-        decay_rate * work[10:12, :] + g_next * g_next + present * damping + (1.0 - present)
-    )
-    g1 = jnp.concatenate([g[1:2], g_next[0:1]])
-    d1 = jnp.concatenate([d[1:2], d_next[0:1]])
-    f_last = (edge(6, 7, 1) + g[1:2] * g_next[0:1]) * present[0:1]
-    f = jnp.concatenate([edge(6, 6, 1), f_last])
-    s = (edge(7, 6, 2) + g * g_next) * present
-    f_next = decay_rate * work[12:13, :] + g_next[0:1] * g_next[1:2]
-    c = jnp.concatenate([f_last, f_next])
-    v, p1, _ = solved(g, g1, g_next, d, d1, d_next, f, c, s)
     tiles[8:16, :] = edges[8 * TILE : 9 * TILE, :]
-    tiles[14:15, :] = v[0:1] - edge(9, 5, 1) - edge(10, 4, 1)
-    tiles[15:16, :] = v[1:2] - p1[0:1] - edge(10, 5, 1)
     tiles[16:24, :] = edges[6 * TILE : 7 * TILE, :]
-    tiles[23:24, :] = f_last
     tiles[24:32, :] = edges[7 * TILE : 8 * TILE, :]
-    tiles[30:32, :] = s
+    rest = other if scale != 1.0 else None
+    even = lax.rem(lax.axis_index("fsdp"), 2) == 0
+
+    @pl.when(even)
+    def _():
+        lower(scale, edges, far, rest, tiles)
+        upper(scale, shards, edges, near, None, tiles)
+
+    @pl.when(jnp.logical_not(even))
+    def _():
+        lower(scale, edges, near, None, tiles)
+        upper(scale, shards, edges, far, rest, tiles)
 
     copies = [
         pltpu.make_async_copy(tiles.at[0:8, :], outs[0].at[0:TILE, :], sems.at[0]),
@@ -254,6 +219,57 @@
         copy.start()
     for copy in copies:
         copy.wait()
+
+
+def neighbour(scale, block, rest):
+    g = [block[k : k + 1, :] for k in range(2)]
+    if rest is not None:
+        g = [(g[k] + rest[k : k + 1, :]) * scale for k in range(2)]
+    d = [decay_rate * block[k + 2 : k + 3, :] + g[k] * g[k] + damping for k in range(2)]
+    f = decay_rate * block[4:5, :] + g[0] * g[1]
+    return g, d, f
+
+
+def lower(scale, edges, block, rest, tiles):
+    def edge(k, at):
+        return edges[k * TILE + at : k * TILE + at + 1, :]
+
+    (ga, gb), (da, db), fa = neighbour(scale, block, rest)
+    g0, g1 = edge(0, 0), edge(0, 1)
+    d0, d1 = edge(1, 0) + damping, edge(1, 1) + damping
+    f0 = edge(2, 0)
+    fb = decay_rate * block[5:6, :] + gb * g0
+    sa = decay_rate * block[6:7, :] + ga * g0
+    sb = decay_rate * block[7:8, :] + gb * g1
+    _, _, far_a = solved(ga, gb, g0, da, db, d0, fa, fb, sa)
+    _, near_b, far_b = solved(gb, g0, g1, db, d0, d1, fb, f0, sb)
+    none = lax.axis_index("fsdp") == 0
+    tiles[0:1, :] = edge(3, 0) - jnp.where(none, 0.0, near_b) - jnp.where(none, 0.0, far_a)
+    tiles[1:2, :] = edge(3, 1) - jnp.where(none, 0.0, far_b)
+
+
+def upper(scale, shards, edges, block, rest, tiles):
+    def edge(k, at):
+        return edges[k * TILE + at : k * TILE + at + 1, :]
+
+    none = lax.axis_index("fsdp") == shards - 1
+    (gp, gq), (dp, dq), fp = neighbour(scale, block, rest)
+    gp, gq = jnp.where(none, 0.0, gp), jnp.where(none, 0.0, gq)
+    dp, dq = jnp.where(none, 1.0, dp), jnp.where(none, 1.0, dq)
+    fp = jnp.where(none, 0.0, fp)
+    gx, gy = edge(4, 6), edge(4, 7)
+    dx, dy = edge(5, 6) + damping, edge(5, 7) + damping
+    fx = edge(6, 6)
+    fy = jnp.where(none, 0.0, edge(6, 7) + gy * gp)
+    sx = jnp.where(none, 0.0, edge(7, 6) + gx * gp)
+    sy = jnp.where(none, 0.0, edge(7, 7) + gy * gq)
+    vx, near_x, _ = solved(gx, gy, gp, dx, dy, dp, fx, fy, sx)
+    vy, _, _ = solved(gy, gp, gq, dy, dp, dq, fy, fp, sy)
+    tiles[14:15, :] = vx - edge(9, 5) - edge(10, 4)
+    tiles[15:16, :] = vy - near_x - edge(10, 5)
+    tiles[23:24, :] = fy
+    tiles[30:31, :] = sx
+    tiles[31:32, :] = sy
 
 
 def trades(shards, low):
@@ -306,9 +322,9 @@
         pieces = [lax.psum(own, "replica") * scale]
         scale = 1.0
         tail = rows - 2
-        ones = jnp.ones((2, width), jnp.float32)
+        unused = jnp.zeros((2, width), jnp.float32)
         last = jnp.concatenate([x[tail:] for x in (*pieces, *stats)])
-        head = jnp.concatenate([x[:2] for x in (*pieces, *stats[:2])] + [ones])
+        head = jnp.concatenate([x[:2] for x in (*pieces, *stats[:2])] + [unused])
         before = lax.ppermute(last, "fsdp", [(i, i + 1) for i in range(shards - 1)])
         after = lax.ppermute(head, "fsdp", [(i + 1, i) for i in range(shards - 1)])
         even = lax.axis_index("fsdp") % 2 == 0
@@ -373,8 +389,7 @@
             out_specs=(hbm,) * 3,
             input_output_aliases={4: 0, 5: 1, 6: 2},
             scratch_shapes=[
-                pltpu.VMEM((16, width), jnp.float32),
-                pltpu.VMEM((32, width), jnp.float32),
+                pltpu.VMEM((4 * TILE, width), jnp.float32),
                 pltpu.SemaphoreType.DMA((4,)),
             ],
             compiler_params=params,

time: 9.08 us -> 9.08 us (level)
  no operation moved by 1% of the time
where the time goes in v1:
time: 9.08 us; the launch traced here: 8.93 us
  starting transfers between devices  3.74 us (41%)
  Pallas kernels  3.72 us (41%)
  between operations  0.74 us (8%)
  waiting for transfers between devices  0.71 us (8%)
    ppermute x1, starting transfers between devices, body(): far = lax.ppermute(far, axes, trades(shards, 1))  2.17 us
    pallas_call x2, Pallas kernels, inside(): pl.pallas_call(functools.partial(interior, parts, early, scale, rows, chu...  1.39 us
    ppermute x2, starting transfers between devices, swap(): return lax.ppermute(block, 'replica', [(0, 1), (1, 0)])  0.91 us
    pallas_call x1, Pallas kernels, body(): pl.pallas_call(functools.partial(store, rows, chunk), out_shape=shape, in...  0.81 us
    pallas_call x1, Pallas kernels, body(): pl.pallas_call(functools.partial(collect, rows), out_shape=tile, in_specs...  0.77 us
    pallas_call x2, Pallas kernels, patched(): pl.pallas_call(functools.partial(border, rows, shards, scale, turn), out_...  0.73 us
    ppermute x1, starting transfers between devices, body(): near = lax.ppermute(near, axes, trades(shards, 0))  0.66 us
    ppermute x1, waiting for transfers between devices, body(): far = lax.ppermute(far, axes, trades(shards, 1))  0.6 us
  transfers between devices with their start and end apart: 4, of which 2 were waited for; matrix products, arithmetic and copies ran while one was open for 0% of the time, Pallas kernels for 34%

profile of v1, /device:TPU:9, one launch (start us, length us, event | category | flops | bytes accessed | tf_op | source)
XLA Modules:
  0.0 8.9 jit_solution(9834804582136608075)
XLA Ops:
  0.6 0.0 copy-start
  0.6 0.0 copy-start.1
  0.7 0.0 copy-start.2
  0.7 0.0 copy-start.3
  0.7 0.7 %collective-permute-start.1 = (f32[1024,128]{1,0:T(8,128)}, f32[1024,128]{1,0:T(8,128)S(1)}, u32[]{:S(2)}, u32[]{:S(2)}) collective-permute-start(f32[1024,128]{1,0:T(8,128)} %bitcast.1), channel_id=1, source_target_pairs={{0,1},{1,0},{2,3},{3,2},{4,5},{5,4},{6,7},{7,6},{8,9},{9,8},{10,11... | collective-permute-start | bytes 1572872 | tf_op jit(solution)/shard_map/ppermute | solution.py:299
  1.4 0.8 %collect.1 = f32[8,128]{1,0:T(8,128)S(1)} custom-call(f32[1024,128]{1,0:T(8,128)} %bitcast.2, f32[1024,128]{1,0:T(8,128)} %refs_2_.3, f32[1024,128]{1,0:T(8,128)} %refs_3_.3, f32[1024,128]{1,0:T(8,128)} %refs_4_.3), custom_call_target="tpu_custom_call" | custom-call | tf_op jit(solution)/shard_map/collect/pallas_call | solution.py:308
  2.2 2.2 %collective-permute-start = (f32[8,128]{1,0:T(8,128)S(1)}, f32[8,128]{1,0:T(8,128)S(1)}, u32[]{:S(2)}, u32[]{:S(2)}) collective-permute-start(f32[8,128]{1,0:T(8,128)S(1)} %collect.1), channel_id=1, source_target_pairs={{0,1},{1,0},{2,5},{3,4},{4,3},{5,2},{6,9},{7,8},{8,7},{9,6},{10,13... | collective-permute-start | bytes 12296 | tf_op jit(solution)/shard_map/ppermute | solution.py:320
  4.4 0.0 collective-permute-done.1.other.refs_1_
  4.4 0.0 copy-done
  4.4 0.0 copy-done.1
  4.4 0.0 copy-done.2
  4.4 0.0 copy-done.3
  4.4 0.1 %early.1 = (f32[1024,128]{1,0:T(8,128)}, f32[1024,128]{1,0:T(8,128)}, f32[1024,128]{1,0:T(8,128)}, f32[1024,128]{1,0:T(8,128)S(1)}, f32[88,128]{1,0:T(8,128)S(1)}) custom-call(f32[1024,128]{1,0:T(8,128)S(1)} %bitcast.4, f32[1024,128]{1,0:T(8,128)S(1)} %collective-permute-done.1.other.refs_1_, f32[1024,128]{1,0:T(8,128)S(1)} %copy-done.1, ...), custom_call_target="tpu_custom_call" | custom-call | flops 5898240 | bytes 4718592 | tf_op jit(solution)/shard_map/early/pallas_call | solution.py:340
  4.6 0.7 %collective-permute-start.2 = (f32[8,128]{1,0:T(8,128)S(1)}, f32[8,128]{1,0:T(8,128)S(1)}, u32[]{:S(2)}, u32[]{:S(2)}) collective-permute-start(f32[8,128]{1,0:T(8,128)S(1)} %ready.1), channel_id=1, source_target_pairs={{0,3},{1,2},{2,1},{3,0},{4,7},{5,6},{6,5},{7,4},{8,11},{9,10},{10,... | collective-permute-start | bytes 12296 | tf_op jit(solution)/shard_map/ppermute | solution.py:365
  5.2 1.3 %late.1 = (f32[1024,128]{1,0:T(8,128)}, f32[1024,128]{1,0:T(8,128)}, f32[1024,128]{1,0:T(8,128)}, f32[1024,128]{1,0:T(8,128)S(1)}, f32[88,128]{1,0:T(8,128)S(1)}) custom-call(f32[1024,128]{1,0:T(8,128)S(1)} %bitcast.5, ...), custom_call_target="tpu_custom_call", output_to_operand_aliasing={{0}: (5, {}), {1}: (6, {}), {2}: (7, {}), {3}: (8, {}), {4}... | custom-call | flops 5898240 | bytes 4718592 | tf_op jit(solution)/shard_map/late/pallas_call | solution.py:340
  6.5 0.6 %collective-permute-done.refs_2_.refs_3_ = f32[8,128]{1,0:T(8,128)S(1)} collective-permute-done((f32[8,128]{1,0:T(8,128)S(1)}, f32[8,128]{1,0:T(8,128)S(1)}, u32[]{:S(2)}, u32[]{:S(2)}) %collective-permute-start) | collective-permute-done | bytes 4128 | tf_op jit(solution)/shard_map/ppermute | solution.py:320
  7.1 0.2 %collective-permute-start.3 = (f32[8,128]{1,0:T(8,128)S(1)}, f32[8,128]{1,0:T(8,128)S(1)}, u32[]{:S(2)}, u32[]{:S(2)}) collective-permute-start(f32[8,128]{1,0:T(8,128)S(1)} %collective-permute-done.refs_2_.refs_3_), channel_id=1, source_target_pairs={{0,1},{1,0},{2,3},{3,2},{4,5},{5,4},{6,7},{7,6},{8,9},{9,8},{10,11... | collective-permute-start | bytes 12296 | tf_op jit(solution)/shard_map/ppermute | solution.py:299
  7.3 0.8 %store.1.refs_4_ = f32[1024,128]{1,0:T(8,128)} custom-call(f32[1024,128]{1,0:T(8,128)S(1)} %get-tuple-element.42.update), custom_call_target="tpu_custom_call" | custom-call | bytes 1048576 | tf_op jit(solution)/shard_map/store/pallas_call | solution.py:371
  8.1 0.0 collective-permute-done.2.refs_1_
  8.1 0.1 border.2
  8.1 0.1 %collective-permute-done.3.refs_3_ = f32[8,128]{1,0:T(8,128)S(1)} collective-permute-done((f32[8,128]{1,0:T(8,128)S(1)}, f32[8,128]{1,0:T(8,128)S(1)}, u32[]{:S(2)}, u32[]{:S(2)}) %collective-permute-start.3) | collective-permute-done | bytes 4128 | tf_op jit(solution)/shard_map/ppermute | solution.py:299
  8.3 0.7 %border.3 = (f32[1024,128]{1,0:T(8,128)}, f32[1024,128]{1,0:T(8,128)}, f32[1024,128]{1,0:T(8,128)}) custom-call(f32[88,128]{1,0:T(8,128)S(1)} %get-tuple-element.39.refs_0_, f32[8,128]{1,0:T(8,128)S(1)} %collective-permute-done.2.refs_1_, ...), custom_call_target="tpu_custom_call", output_to_operand_aliasing={{0}: (4, {}), {1}: (5, {}), {2}: (6, {})} | custom-call | tf_op jit(solution)/shard_map/border/pallas_call | solution.py:385
  (1 shorter events, 0.0 us)
Async XLA Ops:
  0.6 3.7 %copy-start = (f32[1,1024,128]{2,1,0:T(8,128)S(1)}, f32[1,1024,128]{2,1,0:T(8,128)}, u32[]{:S(2)}) copy-start(f32[1,1024,128]{2,1,0:T(8,128)} %param.4) | copy-start | bytes 1572868
  0.6 3.7 %copy-start.1 = (f32[1024,128]{1,0:T(8,128)S(1)}, f32[1024,128]{1,0:T(8,128)}, u32[]{:S(2)}) copy-start(f32[1024,128]{1,0:T(8,128)} %refs_2_.3) | copy-start | bytes 1572868
  0.7 3.7 %copy-start.2 = (f32[1024,128]{1,0:T(8,128)S(1)}, f32[1024,128]{1,0:T(8,128)}, u32[]{:S(2)}) copy-start(f32[1024,128]{1,0:T(8,128)} %refs_3_.3) | copy-start | bytes 1572868
  0.7 3.7 %copy-start.3 = (f32[1024,128]{1,0:T(8,128)S(1)}, f32[1024,128]{1,0:T(8,128)}, u32[]{:S(2)}) copy-start(f32[1024,128]{1,0:T(8,128)} %refs_4_.3) | copy-start | bytes 1572868
  0.7 3.7 %collective-permute-start.1 = (f32[1024,128]{1,0:T(8,128)}, f32[1024,128]{1,0:T(8,128)S(1)}, u32[]{:S(2)}, u32[]{:S(2)}) collective-permute-start(f32[1024,128]{1,0:T(8,128)} %bitcast.1), channel_id=1, source_target_pairs={{0,1},{1,0},{2,3},{3,2},{4,5},{5,4},{6,7},{7,6},{8,9},{9,8},{10,11... | collective-permute-start | bytes 1572872 | tf_op jit(solution)/shard_map/ppermute | solution.py:299
  2.2 4.9 %collective-permute-start = (f32[8,128]{1,0:T(8,128)S(1)}, f32[8,128]{1,0:T(8,128)S(1)}, u32[]{:S(2)}, u32[]{:S(2)}) collective-permute-start(f32[8,128]{1,0:T(8,128)S(1)} %collect.1), channel_id=1, source_target_pairs={{0,1},{1,0},{2,5},{3,4},{4,3},{5,2},{6,9},{7,8},{8,7},{9,6},{10,13... | collective-permute-start | bytes 12296 | tf_op jit(solution)/shard_map/ppermute | solution.py:320
  4.6 3.5 %collective-permute-start.2 = (f32[8,128]{1,0:T(8,128)S(1)}, f32[8,128]{1,0:T(8,128)S(1)}, u32[]{:S(2)}, u32[]{:S(2)}) collective-permute-start(f32[8,128]{1,0:T(8,128)S(1)} %ready.1), channel_id=1, source_target_pairs={{0,3},{1,2},{2,1},{3,0},{4,7},{5,6},{6,5},{7,4},{8,11},{9,10},{10,... | collective-permute-start | bytes 12296 | tf_op jit(solution)/shard_map/ppermute | solution.py:365
  7.1 1.2 %collective-permute-start.3 = (f32[8,128]{1,0:T(8,128)S(1)}, f32[8,128]{1,0:T(8,128)S(1)}, u32[]{:S(2)}, u32[]{:S(2)}) collective-permute-start(f32[8,128]{1,0:T(8,128)S(1)} %collective-permute-done.refs_2_.refs_3_), channel_id=1, source_target_pairs={{0,1},{1,0},{2,3},{3,2},{4,5},{5,4},{6,7},{7,6},{8,9},{9,8},{10,11... | collective-permute-start | bytes 12296 | tf_op jit(solution)/shard_map/ppermute | solution.py:299
